TPU v7x, 32 devices: a whole 2x2x4 slice. The times are simulated.
32 devices in a mesh: rep: 4 (over z), fsdp: 8 (over y, x, core).
Axes of the slice: x: 2, y: 2, z: 4, core: 2. Of those that a mesh axis runs over, the one named last changes fastest.
Arguments:
- layer_input: bfloat16 [16, 1024, 768], P('rep', 'fsdp'), may hold values from -40 to 40
- positions: int32 [16, 1024], P('rep', 'fsdp'), may hold values from 0 to 1023, as said below
- cotangent: bfloat16 [16, 1024, 768], P('rep', 'fsdp'), may hold values from -6 to 6
- w_qkv: bfloat16 [768, 2304], P('fsdp'), may hold values from -4 to 4
- w_out: bfloat16 [768, 768], P('fsdp'), may hold values from -1.75 to 1.75
- w_up: bfloat16 [768, 3072], P('fsdp'), may hold values from -0.21875 to 0.21875
- w_down: bfloat16 [768, 3072], P('fsdp'), may hold values from -0.109375 to 0.109375
- ln1_gain: bfloat16 [768], P('fsdp'), may hold values from 0.5 to 1.5
- ln1_bias: bfloat16 [768], P('fsdp'), may hold values from -1.5 to 1.5
- ln2_gain: bfloat16 [768], P('fsdp'), may hold values from 0.5 to 1.5
- ln2_bias: bfloat16 [768], P('fsdp'), may hold values from -1.5 to 1.5
- qkv_bias: bfloat16 [2304], P('fsdp'), may hold values from -2.5 to 2.5
- out_bias: bfloat16 [768], P('fsdp'), may hold values from -2.5 to 2.5
- up_bias: bfloat16 [3072], P('fsdp'), may hold values from -2.5 to 2.5
- down_bias: bfloat16 [768], P('fsdp'), may hold values from -2.5 to 2.5
Outputs:
- output: bfloat16 [16, 1024, 768], P('rep', 'fsdp')
- grad_input: bfloat16 [16, 1024, 768], P('rep', 'fsdp')
- grad_w_qkv: float32 [768, 2304], P('fsdp')
- grad_w_out: float32 [768, 768], P('fsdp')
- grad_w_up: float32 [768, 3072], P('fsdp')
- grad_w_down: float32 [768, 3072], P('fsdp')
- grad_ln1_gain: float32 [768], P('fsdp')
- grad_ln1_bias: float32 [768], P('fsdp')
- grad_ln2_gain: float32 [768], P('fsdp')
- grad_ln2_bias: float32 [768], P('fsdp')
- grad_qkv_bias: float32 [2304], P('fsdp')
- grad_out_bias: float32 [768], P('fsdp')
- grad_up_bias: float32 [3072], P('fsdp')
- grad_down_bias: float32 [768], P('fsdp')
Inputs may be any that keep to these rules, and one draw needn't show every extreme that they name: positions[s, 0] is 0, and each later positions[s, t] is either 0 or positions[s, t - 1] + 1; sequence 0 is one document of 1024 tokens.
All inputs are finite; a program needn't handle non-finite values.
Results may differ from a plain program's by a relative error of at most 0.0093.
Values may be sent and summed in bfloat16 or wider, within the bound.
No kernel may reach another device: no remote copies, remote signals or barrier semaphores. Data moves between devices by JAX's collectives and lax.ppermute only.
A program may use at most 320 MiB of HBM per device.

v0:
```python
import jax
import jax.numpy as jnp
from jax import lax
from jax.sharding import PartitionSpec as P

H = 12
HD = 64
ROT = 16
EPS = 1e-05
NEG = -1e30


def norm_rows(values, gain, shift):
    mean = jnp.mean(values, axis=-1, keepdims=True)
    centred = values - mean
    spread = jnp.mean(centred * centred, axis=-1, keepdims=True)
    return centred * lax.rsqrt(spread + EPS) * gain + shift


def rotate(values, cosine, sine):
    half = ROT // 2
    head = values[..., :ROT]
    turned = jnp.concatenate([-head[..., half:], head[..., :half]], axis=-1)
    return jnp.concatenate([head * cosine + turned * sine, values[..., ROT:]], axis=-1)


def angles(positions):
    inverse = 10000.0 ** (-jnp.arange(0, ROT, 2, dtype=jnp.float32) / ROT)
    phase = positions.astype(jnp.float32)[..., None] * inverse
    phase = jnp.concatenate([phase, phase], axis=-1)[..., None, :]
    return (jnp.cos(phase), jnp.sin(phase))


def on_device(
    layer_input,
    positions,
    cotangent,
    w_qkv,
    w_out,
    w_up,
    w_down,
    ln1_gain,
    ln1_bias,
    ln2_gain,
    ln2_bias,
    qkv_bias,
    out_bias,
    up_bias,
    down_bias,
):
    seq_count, span_len, width = layer_input.shape
    shard_count = lax.axis_size("fsdp")
    shard_index = lax.axis_index("fsdp")
    row_count = seq_count * span_len
    qkv_cols = w_qkv.shape[1]
    hidden_cols = w_up.shape[1]
    vectors = (
        lax.all_gather(ln1_gain, "fsdp", axis=0, tiled=True),
        lax.all_gather(ln1_bias, "fsdp", axis=0, tiled=True),
        lax.all_gather(ln2_gain, "fsdp", axis=0, tiled=True),
        lax.all_gather(ln2_bias, "fsdp", axis=0, tiled=True),
        lax.all_gather(qkv_bias, "fsdp", axis=0, tiled=True),
        lax.all_gather(out_bias, "fsdp", axis=0, tiled=True),
        lax.all_gather(up_bias, "fsdp", axis=0, tiled=True),
        lax.all_gather(down_bias, "fsdp", axis=0, tiled=True),
    )
    gain_one, shift_one, gain_two, shift_two, bias_qkv, bias_out, bias_up, bias_down = [
        v.astype(jnp.float32) for v in vectors
    ]
    source = layer_input.reshape(row_count, width).astype(jnp.float32)
    normed_one, pull_one = jax.vjp(norm_rows, source, gain_one, shift_one)
    normed_two, pull_two = jax.vjp(norm_rows, source, gain_two, shift_two)
    input_one = normed_one.astype(jnp.bfloat16)
    input_two = normed_two.astype(jnp.bfloat16)
    pieces = (
        lax.all_gather(w_qkv, "fsdp", axis=0, tiled=True),
        lax.all_gather(w_up, "fsdp", axis=0, tiled=True),
    )
    count = pieces[0].shape[0]
    qkv_sum = jnp.dot(input_one, pieces[0], preferred_element_type=jnp.float32)
    up_sum = jnp.dot(input_two, pieces[1], preferred_element_type=jnp.float32)
    qkv_full = qkv_sum + bias_qkv
    up_full = up_sum + bias_up
    cosine, sine = angles(positions)

    def turn_all(packed):
        shaped = packed.reshape(seq_count, span_len, 3, H, HD)
        return (
            rotate(shaped[:, :, 0], cosine, sine),
            rotate(shaped[:, :, 1], cosine, sine),
            shaped[:, :, 2],
        )

    turned, pull_turn = jax.vjp(turn_all, qkv_full)
    query_low = turned[0].astype(jnp.bfloat16)
    key_low = turned[1].astype(jnp.bfloat16)
    value_low = turned[2].astype(jnp.bfloat16)
    key_flat = key_low.reshape(seq_count, span_len, width)
    value_flat = value_low.reshape(seq_count, span_len, width)
    query_index = shard_index * span_len + jnp.arange(span_len, dtype=jnp.int32)
    first_seen = query_index[None, :] - positions

    def scores_with(key_piece):
        count = key_piece.shape[1]
        keys = key_piece.reshape(seq_count, count, H, HD)
        raw = (
            jnp.einsum("sqhd,skhd->shqk", query_low, keys, preferred_element_type=jnp.float32)
            * 0.125
        )
        key_index = jnp.arange(count, dtype=jnp.int32)
        seen = (key_index[None, None, :] <= query_index[None, :, None]) & (
            key_index[None, None, :] >= first_seen[:, :, None]
        )
        return (raw, seen[:, None])

    start_top = jnp.full((seq_count, H, span_len), NEG, jnp.float32)
    raw, seen = scores_with(lax.all_gather(key_flat, "fsdp", axis=1, tiled=True))
    masked = jnp.where(seen, raw, NEG)
    new_top = jnp.maximum(start_top, jnp.max(masked, axis=-1))
    weights = jnp.where(seen, jnp.exp(masked - new_top[..., None]), 0.0)
    total = jnp.sum(weights, axis=-1)
    log_total = new_top + jnp.log(total)
    pieces = (
        lax.all_gather(key_flat, "fsdp", axis=1, tiled=True),
        lax.all_gather(value_flat, "fsdp", axis=1, tiled=True),
    )
    raw, seen = scores_with(pieces[0])
    count = pieces[1].shape[1]
    values = pieces[1].reshape(seq_count, count, H, HD)
    probs = jnp.where(seen, jnp.exp(raw - log_total[..., None]), 0.0)
    probs_low = probs.astype(jnp.bfloat16)
    residue = (probs - probs_low.astype(jnp.float32)).astype(jnp.bfloat16)
    mixed_sum = jnp.einsum("shqk,skhd->sqhd", probs_low, values, preferred_element_type=jnp.float32)
    residue_sum = jnp.einsum("shqk,skhd->sqhd", residue, values, preferred_element_type=jnp.float32)
    attended = mixed_sum.reshape(row_count, width).astype(jnp.bfloat16)
    hidden = jax.nn.gelu(up_full, approximate=False).astype(jnp.bfloat16)
    pieces = (
        lax.all_gather(w_out, "fsdp", axis=0, tiled=True),
        lax.all_gather(w_down, "fsdp", axis=0, tiled=True),
    )
    columns = jnp.einsum("rk,ck->rc", attended, pieces[0], preferred_element_type=jnp.float32)
    columns = columns + jnp.einsum(
        "rk,ck->rc", hidden, pieces[1], preferred_element_type=jnp.float32
    )
    output = (
        (source + columns + bias_out + bias_down).astype(jnp.bfloat16).reshape(layer_input.shape)
    )
    grad_out = cotangent.reshape(row_count, width)
    pieces = (
        lax.all_gather(w_out, "fsdp", axis=0, tiled=True),
        lax.all_gather(w_down, "fsdp", axis=0, tiled=True),
    )
    count = pieces[0].shape[0]
    grad_attended = jnp.dot(grad_out, pieces[0], preferred_element_type=jnp.float32)
    grad_hidden = jnp.dot(grad_out, pieces[1], preferred_element_type=jnp.float32)
    grad_mixed = grad_attended.astype(jnp.bfloat16)
    gelu_value, pull_gelu = jax.vjp(lambda v: jax.nn.gelu(v, approximate=False), up_full)
    grad_up = pull_gelu(grad_hidden)[0].astype(jnp.bfloat16)
    grad_heads = grad_mixed.reshape(seq_count, span_len, H, HD)
    carried = jnp.sum(grad_heads.astype(jnp.float32) * (mixed_sum + residue_sum), axis=-1)
    carried_rows = jnp.transpose(carried, (0, 2, 1))
    pieces = (
        lax.all_gather(key_flat, "fsdp", axis=1, tiled=True),
        lax.all_gather(value_flat, "fsdp", axis=1, tiled=True),
    )
    raw, seen = scores_with(pieces[0])
    count = pieces[0].shape[1]
    keys = pieces[0].reshape(seq_count, count, H, HD)
    values = pieces[1].reshape(seq_count, count, H, HD)
    probs = jnp.where(seen, jnp.exp(raw - log_total[..., None]), 0.0)
    probs_low = probs.astype(jnp.bfloat16)
    grad_probs = jnp.einsum(
        "sqhd,skhd->shqk", grad_heads, values, preferred_element_type=jnp.float32
    )
    grad_scores = (probs * (grad_probs - carried_rows[..., None])).astype(jnp.bfloat16)
    grad_query = jnp.einsum(
        "shqk,skhd->sqhd", grad_scores, keys, preferred_element_type=jnp.float32
    )
    key_part = jnp.einsum(
        "shqk,sqhd->skhd", grad_scores, query_low, preferred_element_type=jnp.float32
    )
    value_part = jnp.einsum(
        "shqk,sqhd->skhd", probs_low, grad_heads, preferred_element_type=jnp.float32
    )
    both = jnp.concatenate(
        [key_part.reshape(seq_count, count, width), value_part.reshape(seq_count, count, width)],
        axis=2,
    )
    key_terms = both
    grad_query, key_terms = (grad_query, key_terms)
    grad_query = grad_query * 0.125
    key_owned = lax.psum_scatter(key_terms, "fsdp", scatter_dimension=1, tiled=True)
    grad_key = key_owned[..., :width].reshape(seq_count, span_len, H, HD) * 0.125
    grad_value = key_owned[..., width:].reshape(seq_count, span_len, H, HD)
    grad_qkv = pull_turn((grad_query, grad_key, grad_value))[0].astype(jnp.bfloat16)
    pieces = (
        lax.all_gather(w_qkv, "fsdp", axis=0, tiled=True),
        lax.all_gather(w_up, "fsdp", axis=0, tiled=True),
    )
    columns_one = jnp.einsum("rk,ck->rc", grad_qkv, pieces[0], preferred_element_type=jnp.float32)
    columns_two = jnp.einsum("rk,ck->rc", grad_up, pieces[1], preferred_element_type=jnp.float32)
    grad_source_one, grad_gain_one, grad_shift_one = pull_one(columns_one)
    grad_source_two, grad_gain_two, grad_shift_two = pull_two(columns_two)
    grad_out_float = grad_out.astype(jnp.float32)
    grad_input = (
        (grad_out_float + grad_source_one + grad_source_two)
        .astype(jnp.bfloat16)
        .reshape(layer_input.shape)
    )
    grad_out_total = jnp.sum(grad_out_float, axis=0)
    local_vectors = (
        grad_gain_one,
        grad_shift_one,
        grad_gain_two,
        grad_shift_two,
        jnp.sum(grad_qkv.astype(jnp.float32), axis=0),
        grad_out_total,
        jnp.sum(grad_up.astype(jnp.float32), axis=0),
    )
    summed = lax.psum(
        (
            local_vectors[0],
            local_vectors[1],
            local_vectors[2],
            local_vectors[3],
            local_vectors[4],
            local_vectors[5],
            local_vectors[6],
        ),
        ("rep", "fsdp"),
    )
    owned_vectors = [
        lax.dynamic_slice_in_dim(
            v, shard_index * (v.shape[0] // shard_count), v.shape[0] // shard_count
        )
        for v in summed
    ]
    owned = lax.psum_scatter(
        jnp.concatenate(
            [
                jnp.einsum("rc,rk->ck", input_one, grad_qkv, preferred_element_type=jnp.float32),
                jnp.einsum("rc,rk->ck", grad_out, attended, preferred_element_type=jnp.float32),
                jnp.einsum("rc,rk->ck", input_two, grad_up, preferred_element_type=jnp.float32),
                jnp.einsum("rc,rk->ck", grad_out, hidden, preferred_element_type=jnp.float32),
            ],
            axis=1,
        ),
        "fsdp",
        scatter_dimension=0,
        tiled=True,
    )
    owned = lax.psum(owned, "rep")
    edge_two = qkv_cols + width
    edge_three = edge_two + hidden_cols
    grad_w_qkv = owned[:, :qkv_cols]
    grad_w_out = owned[:, qkv_cols:edge_two]
    grad_w_up = owned[:, edge_two:edge_three]
    grad_w_down = owned[:, edge_three:]
    return (
        output,
        grad_input,
        grad_w_qkv,
        grad_w_out,
        grad_w_up,
        grad_w_down,
        owned_vectors[0],
        owned_vectors[1],
        owned_vectors[2],
        owned_vectors[3],
        owned_vectors[4],
        owned_vectors[5],
        owned_vectors[6],
        owned_vectors[5],
    )


def solution(mesh):
    return jax.shard_map(
        on_device,
        mesh=mesh,
        in_specs=(
            P("rep", "fsdp", None),
            P("rep", "fsdp"),
            P("rep", "fsdp", None),
            P("fsdp", None),
            P("fsdp", None),
            P("fsdp", None),
            P("fsdp", None),
            P("fsdp"),
            P("fsdp"),
            P("fsdp"),
            P("fsdp"),
            P("fsdp"),
            P("fsdp"),
            P("fsdp"),
            P("fsdp"),
        ),
        out_specs=(
            P("rep", "fsdp", None),
            P("rep", "fsdp", None),
            P("fsdp", None),
            P("fsdp", None),
            P("fsdp", None),
            P("fsdp", None),
            P("fsdp"),
            P("fsdp"),
            P("fsdp"),
            P("fsdp"),
            P("fsdp"),
            P("fsdp"),
            P("fsdp"),
            P("fsdp"),
        ),
        check_vma=False,
    )
```

profile of v0, /device:TPU:0, one launch (start us, length us, event | category | flops | bytes accessed | tf_op | source)
XLA Modules:
  0.0 780.7 jit_solution(14124956346842506521)
XLA Ops:
  21.0 26.5 %all-reduce.19 = (bf16[768]{0:T(1024)(128)(2,1)S(1)}, bf16[768]{0:T(1024)(128)(2,1)S(1)}, bf16[768]{0:T(1024)(128)(2,1)}, bf16[768]{0:T(1024)(128)(2,1)}, bf16[7...) all-reduce(bf16[768]{0:T(1024)(128)(2,1)S(1)} %dynamic-update-slice, ...), channel_id=1, replica_groups=mesh['rep'=4,'fsdp'=8] {'fsdp'}, use_global_device_ids=true, to_apply=%add.15 | all-reduce | flops 6912 | bytes 27648
  49.2 6.1 convolution_add_fusion
  55.4 6.2 copy.46
  61.5 6.3 reshape.249
  84.6 37.4 %all-gather.12.cloned.1.call-done = bf16[4,1024,768]{1,2,0:T(8,128)(2,1)} async-done(((bf16[4,128,768]{1,2,0:T(8,128)(2,1)}), bf16[4,1024,768]{1,2,0:T(8,128)(2,1)}) %all-gather.12.cloned.1.call-update) | async-done | bytes 6291472 | tf_op jit(solution)/shard_map/all_gather | solution.py:124
  121.9 12.9 %select_reduce_fusion.1 = (f32[4,12,128]{2,1,0:T(8,128)S(1)}, f32[4,12,128,1024]{3,2,1,0:T(8,128)}) fusion(pred[4,128,1024]{2,1,0:T(8,128)(4,1)S(1)} %fusion.13, bf16[4,1024,12,64]{1,3,2,0:T(8,128)(2,1)} %bitcast.164, bf16[4,128,12,48]{1,3,2,0:T(8,128)(2,1)S(1)} %slice.110, bf16[4,128,12,16]{1,3,2,0:T(8,128)(2,1)S(1)} %get-tuple-element.61), kind=kOutput, calls=%fused_computation.6 | convolution fusion | flops 825747456 | bytes 32792576 | tf_op jit(solution)/shard_map/sqhd,skhd->shqk/dot_general | solution.py:107
  134.9 12.2 %select_reduce_fusion = f32[4,12,128]{2,1,0:T(8,128)S(1)} fusion(f32[4,12,128,1024]{3,2,1,0:T(8,128)} %get-tuple-element.76, f32[4,12,128]{2,1,0:T(8,128)S(1)} %broadcast_maximum_fusion, pred[4,128,1024]{2,1,0:T(8,128)(4,1)S(1)} %fusion.13), kind=kLoop, calls=%fused_computation.5 | loop fusion | flops 31451136 | bytes 25739264 | tf_op jit(solution)/shard_map/reduce_sum | solution.py:121
  147.1 23.9 %all-gather.10.cloned.1.call-done = bf16[4,1024,768]{1,2,0:T(8,128)(2,1)} async-done(((bf16[4,128,768]{1,2,0:T(8,128)(2,1)}), bf16[4,1024,768]{1,2,0:T(8,128)(2,1)}) %all-gather.10.cloned.1.call-update) | async-done | bytes 6291472 | tf_op jit(solution)/shard_map/all_gather | solution.py:125
  170.9 14.2 %fusion.58 = f32[4,12,64,128]{3,2,1,0:T(8,128)} fusion(bf16[4,1024,12,64]{1,3,2,0:T(8,128)(2,1)} %bitcast.190, f32[4,12,128,1024]{3,2,1,0:T(8,128)} %get-tuple-element.76, f32[4,12,128]{2,1,0:T(8,128)S(1)} %log_add_fusion, pred[4,128,1024]{2,1,0:T(8,128)(4,1)S(1)} %fusion.13), kind=kOutput, calls=%fused_computation.110 | convolution fusion | flops 830472192 | bytes 33579008 | tf_op jit(solution)/shard_map/shqk,skhd->sqhd/dot_general | solution.py:133
  185.2 15.0 %fusion.16 = f32[4,128,12]{1,2,0:T(8,128)S(1)} fusion(f32[4,12,64,128]{3,2,1,0:T(8,128)} %fusion.58, bf16[4,1024,12,64]{1,3,2,0:T(8,128)(2,1)} %bitcast.191, f32[4,12,128,1024]{3,2,1,0:T(8,128)} %get-tuple-element.76, f32[4,12,128]{2,1,0:T(8,128)S(1)} %log_add_fusion, pred[4,128,1024]{2,1,0:T(8,128)(4,1)S(1)} %fusion.13, bf16[4,128,12,64]{1,0,3,2:T(4,128)(2,1)} %reshape.254), kind=kOutput, calls=%fused_computation.48 | convolution fusion | flops 850913280 | bytes 34390016 | tf_op jit(solution)/shard_map/shqk,skhd->sqhd/dot_general | solution.py:134
  200.2 20.5 %multiply_convert_fusion = bf16[4,12,128,1024]{3,2,1,0:T(8,128)(2,1)} fusion(f32[4,12,128,1024]{3,2,1,0:T(8,128)} %get-tuple-element.76, f32[4,12,128]{2,1,0:T(8,128)S(1)} %bitcast.194, f32[4,12,128]{2,1,0:T(8,128)S(1)} %log_add_fusion, pred[4,128,1024]{2,1,0:T(8,128)(4,1)S(1)} %fusion.13, bf16[4,1024,12,64]{1,3,2,0:T(8,128)(2,1)} %bitcast.192, ...), kind=kOutput, calls=%fused_computation.2 | convolution fusion | flops 843055104 | bytes 45400064 | tf_op jit(solution)/shard_map/sqhd,skhd->shqk/dot_general | solution.py:172
  220.6 11.1 %fusion.50 = f32[4,12,64,1024]{3,2,1,0:T(8,128)} fusion(bf16[4,12,128,1024]{3,2,1,0:T(8,128)(2,1)} %multiply_convert_fusion, bf16[4,128,12,48]{1,3,2,0:T(8,128)(2,1)S(1)} %slice.110, bf16[4,128,12,16]{1,3,2,0:T(8,128)(2,1)S(1)} %get-tuple-element.61), kind=kOutput, calls=%fused_computation.98 | convolution fusion | flops 806879232 | bytes 25952256 | tf_op jit(solution)/shard_map/shqk,sqhd->skhd/dot_general | solution.py:179
  231.8 14.8 %fusion.47 = f32[4,12,64,1024]{3,2,1,0:T(8,128)} fusion(bf16[4,128,12,64]{1,0,3,2:T(4,128)(2,1)S(1)} %copy-done.12, f32[4,12,128,1024]{3,2,1,0:T(8,128)} %get-tuple-element.76, f32[4,12,128]{2,1,0:T(8,128)S(1)} %log_add_fusion, pred[4,128,1024]{2,1,0:T(8,128)(4,1)S(1)} %fusion.13), kind=kOutput, calls=%fused_computation.94 | convolution fusion | flops 830472192 | bytes 39084032 | tf_op jit(solution)/shard_map/shqk,sqhd->skhd/dot_general | solution.py:182
  246.5 18.8 %pad_maximum_fusion.1 = f32[4,1024,1536]{1,2,0:T(8,128)} fusion(f32[4,1024,768]{1,2,0:T(8,128)} %bitcast.163, f32[4,1024,768]{1,2,0:T(8,128)} %bitcast.162), kind=kLoop, calls=%fused_computation.1 | loop fusion | flops 6291456 | bytes 50331648 | tf_op jit(solution)/shard_map/concatenate | solution.py:185
  266.0 9.4 %all-gather = bf16[8,1,384]{2,1,0:T(2,128)(2,1)S(1)} all-gather(bf16[1,1,384]{2,1,0:T(2,128)(2,1)S(1)} %reshape.280), channel_id=1, replica_groups=mesh['rep'=4,'fsdp'=8] {'fsdp'}, dimensions={0}, use_global_device_ids=true | all-gather | bytes 6912 | tf_op jit(solution)/shard_map/all_gather | solution.py:64
  276.7 8.9 %fusion.83 = f32[512,3072]{1,0:T(8,128)} fusion(bf16[512,768]{1,0:T(8,128)(2,1)S(1)} %get-tuple-element.54, bf16[768,3072]{1,0:T(8,128)(2,1)} %all-gather.16.cloned.1.call-done), kind=kOutput, calls=%fused_computation.154 | convolution fusion | flops 2415919104 | bytes 11796480 | tf_op jit(solution)/shard_map/dot_general | solution.py:81
  285.6 19.4 %convert_reduce_fusion = (f32[3072]{0:T(1024)S(1)}, bf16[512,3072]{1,0:T(8,128)(2,1)S(1)}, f32[512,3072]{1,0:T(8,128)S(1)}) fusion(f32[512,3072]{1,0:T(8,128)} %fusion.83, f32[3072]{0:T(1024)S(1)} %bitcast.188, bf16[512,768]{1,0:T(8,128)(2,1)S(1)} %bitcast.170, bf16[768,3072]{1,0:T(8,128)(2,1)} %all-gather.18.cloned.1.call-done), kind=kOutput, calls=%fused_computation.12 | convolution fusion | flops 2533880832 | bytes 21258240 | tf_op jit(solution)/shard_map/dot_general | solution.py:155
  308.2 7.8 convolution_bitcast_fusion
  321.2 11.3 %multiply_bitcast_fusion = f32[4,128,12,64]{1,3,2,0:T(8,128)S(1)} fusion(bf16[4,1024,12,64]{1,3,2,0:T(8,128)(2,1)} %bitcast.165, bf16[4,12,128,1024]{3,2,1,0:T(8,128)(2,1)} %multiply_convert_fusion), kind=kOutput, calls=%fused_computation.82 | convolution fusion | flops 805699584 | bytes 20447232 | tf_op jit(solution)/shard_map/shqk,skhd->sqhd/dot_general | solution.py:176
  340.6 82.4 %reduce-scatter.3.cloned.1.call-done = f32[4,128,1536]{1,2,0:T(8,128)} async-done(((f32[4,1024,1536]{1,2,0:T(8,128)}), f32[4,128,1536]{1,2,0:T(8,128)}) %reduce-scatter.3.cloned.1.call-update) | async-done | bytes 3145744 | tf_op jit(solution)/shard_map/reduce_scatter | solution.py:192
  436.1 19.4 %pad_maximum_fusion = f32[768,9216]{1,0:T(8,128)} fusion(f32[768,3072]{1,0:T(8,128)} %convolution_bitcast_fusion, f32[768,3072]{1,0:T(8,128)} %fusion.86, f32[768,768]{1,0:T(8,128)S(1)} %copy.57, f32[768,2304]{1,0:T(8,128)} %fusion.9), kind=kLoop, calls=%fused_computation | loop fusion | flops 21233664 | bytes 56623104 | tf_op jit(solution)/shard_map/concatenate | solution.py:239
  456.4 172.6 %reduce-scatter.5.cloned.1.call-done = f32[96,9216]{1,0:T(8,128)} async-done(((f32[768,9216]{1,0:T(8,128)}), f32[96,9216]{1,0:T(8,128)}) %reduce-scatter.5.cloned.1.call-update) | async-done | bytes 3538960 | tf_op jit(solution)/shard_map/reduce_scatter | solution.py:238
  650.8 44.4 %all-reduce.18 = (f32[768]{0:T(1024)S(1)}, f32[768]{0:T(1024)S(1)}, f32[768]{0:T(1024)S(1)}, f32[768]{0:T(1024)S(1)}, f32[2304]{0:T(1024)S(1)}, /*index=5*/f32[768]{0:T(1024)S(1)}, f32[3072]{0:T(1024)S(1)}) all-reduce(f32[768]{0:T(1024)S(1)} %get-tuple-element.23, ...), channel_id=1, replica_groups=mesh['rep'=4,'fsdp'=8] {'rep','fsdp'}, use_global_device_ids=true, to_apply=%region_13.14 | all-reduce | flops 9216 | bytes 73728 | tf_op jit(solution)/shard_map/psum | solution.py:220
  701.9 64.2 %all-reduce.22.cloned.1.call-done = f32[96,9216]{1,0:T(8,128)} async-done(((f32[96,9216]{1,0:T(8,128)}), f32[96,9216]{1,0:T(8,128)}) %all-reduce.22.cloned.1.call-update) | async-done | bytes 3538960 | tf_op jit(solution)/shard_map/psum | solution.py:252
  (184 shorter events, 98.8 us)
Async XLA Ops:
  7.2 42.0 %all-gather.8.cloned.1.call-start = ((), (), s32[]{:S(2)}) async-start(), calls=%async_computation.2 | async-start | bytes 3981312 | tf_op jit(solution)/shard_map/all_gather | solution.py:76
  7.9 69.8 %all-gather.14.cloned.1.call-start = ((), (), s32[]{:S(2)}) async-start(), calls=%async_computation.5 | async-start | bytes 1327104 | tf_op jit(solution)/shard_map/all_gather | solution.py:138
  8.7 113.3 %all-gather.12.cloned.1.call-start = ((), (), s32[]{:S(2)}) async-start(), calls=%async_computation.4 | async-start | bytes 7077888 | tf_op jit(solution)/shard_map/all_gather | solution.py:124
  10.0 45.3 %copy-start.23 = (f32[512]{0:T(512)}, f32[512]{0:T(512)S(1)}, u32[]{:S(2)}) copy-start(f32[512]{0:T(512)S(1)} %get-tuple-element.73) | copy-start | bytes 6148
  11.6 263.9 %copy-start.27 = (f32[4,128]{1,0:T(4,128)}, f32[4,128]{1,0:T(4,128)S(1)}, u32[]{:S(2)}) copy-start(f32[4,128]{1,0:T(4,128)S(1)} %fusion.28) | copy-start | bytes 6148
  12.5 58.2 %copy-start.15 = (f32[4,128,16]{1,2,0:T(8,128)}, f32[4,128,16]{1,2,0:T(8,128)S(1)}, u32[]{:S(2)}) copy-start(f32[4,128,16]{1,2,0:T(8,128)S(1)} %get-tuple-element.67) | copy-start | bytes 98308
  12.5 58.2 %copy-start.17 = (f32[4,128,16]{1,2,0:T(8,128)}, f32[4,128,16]{1,2,0:T(8,128)S(1)}, u32[]{:S(2)}) copy-start(f32[4,128,16]{1,2,0:T(8,128)S(1)} %get-tuple-element.68) | copy-start | bytes 98308
  47.5 228.0 %copy-start.19 = (f32[768]{0:T(1024)}, f32[768]{0:T(1024)S(1)}, u32[]{:S(2)}) copy-start(f32[768]{0:T(1024)S(1)} %convert_element_type.126) | copy-start | bytes 9220
  47.5 7.9 %copy-start.21 = (f32[768]{0:T(1024)}, f32[768]{0:T(1024)S(1)}, u32[]{:S(2)}) copy-start(f32[768]{0:T(1024)S(1)} %convert_element_type.137) | copy-start | bytes 9220
  47.6 7.8 copy-start.25
  72.8 98.1 %all-gather.10.cloned.1.call-start = ((), (), s32[]{:S(2)}) async-start(), calls=%async_computation.3 | async-start | bytes 7077888 | tf_op jit(solution)/shard_map/all_gather | solution.py:125
  75.6 201.1 %all-gather.16.cloned.1.call-start = ((), (), s32[]{:S(2)}) async-start(), calls=%async_computation.6 | async-start | bytes 5308416 | tf_op jit(solution)/shard_map/all_gather | solution.py:77
  76.2 209.3 %all-gather.18.cloned.1.call-start = ((), (), s32[]{:S(2)}) async-start(), calls=%async_computation.7 | async-start | bytes 5308416 | tf_op jit(solution)/shard_map/all_gather | solution.py:139
  76.8 346.2 %reduce-scatter.3.cloned.1.call-start = ((), (), s32[]{:S(2)}) async-start(), calls=%async_computation.8 | async-start | bytes 28311552 | tf_op jit(solution)/shard_map/reduce_scatter | solution.py:192
  220.6 11.1 %copy-start.12 = (bf16[4,128,12,64]{1,0,3,2:T(4,128)(2,1)S(1)}, bf16[4,128,12,64]{1,0,3,2:T(4,128)(2,1)}, u32[]{:S(2)}) copy-start(bf16[4,128,12,64]{1,0,3,2:T(4,128)(2,1)} %reshape.254) | copy-start | bytes 2359300
  265.3 10.1 %copy-start = (bf16[4,128,768]{2,1,0:T(8,128)(2,1)S(1)}, bf16[4,128,768]{2,1,0:T(8,128)(2,1)}, u32[]{:S(2)}) copy-start(bf16[4,128,768]{2,1,0:T(8,128)(2,1)} %param.15) | copy-start | bytes 2359300
  265.3 363.6 %reduce-scatter.5.cloned.1.call-start = ((), (), s32[]{:S(2)}) async-start(), calls=%async_computation.9 | async-start | bytes 31850496 | tf_op jit(solution)/shard_map/reduce_scatter | solution.py:238
  285.6 19.4 %copy-start.2 = (f32[512,3072]{1,0:T(8,128)S(1)}, f32[512,3072]{1,0:T(8,128)}, u32[]{:S(2)}) copy-start(f32[512,3072]{1,0:T(8,128)} %fusion.83) | copy-start | bytes 18874372
  305.0 11.0 %copy-start.8 = (bf16[512,3072]{1,0:T(8,128)(2,1)}, bf16[512,3072]{1,0:T(8,128)(2,1)S(1)}, u32[]{:S(2)}) copy-start(bf16[512,3072]{1,0:T(8,128)(2,1)S(1)} %get-tuple-element.39) | copy-start | bytes 9437188
  338.5 86.7 %copy-start.18 = (f32[4,128,16]{1,2,0:T(8,128)S(1)}, f32[4,128,16]{1,2,0:T(8,128)}, u32[]{:S(2)}) copy-start(f32[4,128,16]{1,2,0:T(8,128)} %copy-done.17) | copy-start | bytes 98308
  340.6 85.1 %copy-start.16 = (f32[4,128,16]{1,2,0:T(8,128)S(1)}, f32[4,128,16]{1,2,0:T(8,128)}, u32[]{:S(2)}) copy-start(f32[4,128,16]{1,2,0:T(8,128)} %copy-done.15) | copy-start | bytes 98308
  455.5 310.6 %all-reduce.22.cloned.1.call-start = ((), (), s32[]{:S(2)}) async-start(), calls=%async_computation.10 | async-start | bytes 7077888 | tf_op jit(solution)/shard_map/psum | solution.py:252
  642.9 6.5 copy-start.26
  695.3 78.0 %copy-start.33 = (f32[96]{0:T(128)}, f32[96]{0:T(128)S(1)}, u32[]{:S(2)}) copy-start(f32[96]{0:T(128)S(1)} %dynamic_slice.26) | copy-start | bytes 1156
  (20 other events, 58.3 us)
Sparse Core Ops, SparseCore 0:
  9.9 36.8 all-gather.7
  48.7 24.0 all-gather.13
  75.2 46.6 all-gather.11
  124.2 46.6 all-gather.9
  172.7 38.9 all-gather.15
  213.4 38.8 all-gather.17
  265.5 157.4 reduce-scatter.2
  455.7 173.2 reduce-scatter.4
  631.3 134.7 all-reduce.21
where the time goes:
time: 787 us; the launch traced here: 781 us
  waiting for transfers between devices  383 us (49%)
  matrix products  176 us (22%)
  blocking collectives  80.3 us (10%)
  other arithmetic  72.3 us (9%)
  local copies, waits for them, and re-layouts  51.7 us (7%)
  between operations  16.3 us (2%)
    reduce_scatter x1, waiting for transfers between devices, on_device(): lax.psum_scatter(jnp.concatenate([jnp.einsum('rc,rk->ck', input_one, grad...  173 us
    reduce_scatter x1, waiting for transfers between devices, on_device(): lax.psum_scatter(key_terms, 'fsdp', scatter_dimension=1, tiled=True)  82.4 us
    psum x1, waiting for transfers between devices, on_device(): owned = lax.psum(owned, 'rep')  64.2 us
    psum x1, blocking collectives, on_device(): lax.psum((local_vectors[0], local_vectors[1], local_vectors[2], local_vec...  44.4 us
    all_gather x1, waiting for transfers between devices, on_device(): lax.all_gather(key_flat, 'fsdp', axis=1, tiled=True)  37.4 us
    unnamed x1, blocking collectives  26.5 us
    all_gather x1, waiting for transfers between devices, on_device(): lax.all_gather(value_flat, 'fsdp', axis=1, tiled=True)  23.9 us
    dot_general x1, matrix products, on_device(): jnp.einsum('sqhd,skhd->shqk', grad_heads, values, preferred_element_type=...  20.5 us
  transfers between devices with their start and end apart: 9, of which 5 were waited for; matrix products, arithmetic and copies ran while one was open for 33% of the time, Pallas kernels for 0%

commit v1 on v0

--- a/solution.py
+++ b/solution.py
@@ -249,7 +249,11 @@
         scatter_dimension=0,
         tiled=True,
     )
-    owned = lax.psum(owned, "rep")
+    peers, acc = (lax.axis_size("rep"), owned)
+    for far in [1 << k for k in range(peers.bit_length() - 1)]:
+        route = [(i, i ^ far) for i in range(peers)]
+        acc = acc + lax.ppermute(acc, "rep", route)
+    owned = acc
     edge_two = qkv_cols + width
     edge_three = edge_two + hidden_cols
     grad_w_qkv = owned[:, :qkv_cols]

time: 787 us -> 917 us (1.17)
  blocking collectives: 80.3 us -> 194 us
  waiting for transfers between devices: 383 us -> 397 us
    psum x1, blocking collectives: 44.4 us -> 158 us  [on_device(): lax.psum((local_vectors[0], local_vectors[1], local_vectors[2], local_vec...]
    ppermute x0 -> x2, waiting for transfers between devices: none -> 76.9 us  [on_device(): acc = acc + lax.ppermute(acc, 'rep', route)]
    psum x1 -> x0, waiting for transfers between devices: 64.2 us -> none  [on_device(): owned = lax.psum(owned, 'rep')]
  transfers between devices with their start and end apart: 9 -> 10, of which waited for: 5 -> 5; matrix products, arithmetic and copies ran while one was open for 33% -> 27% of each run, Pallas kernels for 0% -> 0%
where the time goes in v1:
time: 917 us; the launch traced here: 910 us
  waiting for transfers between devices  397 us (43%)
  blocking collectives  194 us (21%)
  matrix products  170 us (19%)
  other arithmetic  81.2 us (9%)
  local copies, waits for them, and re-layouts  47.7 us (5%)
  between operations  16.6 us (2%)
    reduce_scatter x1, waiting for transfers between devices, on_device(): lax.psum_scatter(jnp.concatenate([jnp.einsum('rc,rk->ck', input_one, grad...  173 us
    psum x1, blocking collectives, on_device(): lax.psum((local_vectors[0], local_vectors[1], local_vectors[2], local_vec...  158 us
    reduce_scatter x1, waiting for transfers between devices, on_device(): lax.psum_scatter(key_terms, 'fsdp', scatter_dimension=1, tiled=True)  82.4 us
    ppermute x2, waiting for transfers between devices, on_device(): acc = acc + lax.ppermute(acc, 'rep', route)  76.9 us
    all_gather x1, waiting for transfers between devices, on_device(): lax.all_gather(key_flat, 'fsdp', axis=1, tiled=True)  37.4 us
    unnamed x1, blocking collectives  26.5 us
    all_gather x1, waiting for transfers between devices, on_device(): lax.all_gather(value_flat, 'fsdp', axis=1, tiled=True)  23.9 us
    dot_general x1, matrix products, on_device(): jnp.einsum('sqhd,skhd->shqk', grad_heads, values, preferred_element_type=...  20.5 us
  transfers between devices with their start and end apart: 10, of which 5 were waited for; matrix products, arithmetic and copies ran while one was open for 27% of the time, Pallas kernels for 0%

profile of v1, /device:TPU:0, one launch (start us, length us, event | category | flops | bytes accessed | tf_op | source)
XLA Modules:
  0.0 910.2 jit_solution(17819985086039123683)
XLA Ops:
  21.0 26.5 %all-reduce.19 = (bf16[768]{0:T(1024)(128)(2,1)S(1)}, bf16[768]{0:T(1024)(128)(2,1)S(1)}, bf16[768]{0:T(1024)(128)(2,1)}, bf16[768]{0:T(1024)(128)(2,1)}, bf16[7...) all-reduce(bf16[768]{0:T(1024)(128)(2,1)S(1)} %dynamic-update-slice, ...), channel_id=1, replica_groups=mesh['rep'=4,'fsdp'=8] {'fsdp'}, use_global_device_ids=true, to_apply=%add.15 | all-reduce | flops 6912 | bytes 27648
  49.2 6.2 convolution_add_fusion
  55.4 6.2 copy.46
  61.5 6.4 reshape.249
  84.5 37.4 %all-gather.12.cloned.1.call-done = bf16[4,1024,768]{1,2,0:T(8,128)(2,1)} async-done(((bf16[4,128,768]{1,2,0:T(8,128)(2,1)}), bf16[4,1024,768]{1,2,0:T(8,128)(2,1)}) %all-gather.12.cloned.1.call-update) | async-done | bytes 6291472 | tf_op jit(solution)/shard_map/all_gather | solution.py:124
  121.9 12.9 %select_reduce_fusion.1 = (f32[4,12,128]{2,1,0:T(8,128)S(1)}, f32[4,12,128,1024]{3,2,1,0:T(8,128)}) fusion(pred[4,128,1024]{2,1,0:T(8,128)(4,1)S(1)} %fusion.13, bf16[4,1024,12,64]{1,3,2,0:T(8,128)(2,1)} %bitcast.164, bf16[4,128,12,48]{1,3,2,0:T(8,128)(2,1)S(1)} %slice.110, bf16[4,128,12,16]{1,3,2,0:T(8,128)(2,1)S(1)} %get-tuple-element.61), kind=kOutput, calls=%fused_computation.6 | convolution fusion | flops 825747456 | bytes 32792576 | tf_op jit(solution)/shard_map/sqhd,skhd->shqk/dot_general | solution.py:107
  134.9 12.2 %select_reduce_fusion = f32[4,12,128]{2,1,0:T(8,128)S(1)} fusion(f32[4,12,128,1024]{3,2,1,0:T(8,128)} %get-tuple-element.76, f32[4,12,128]{2,1,0:T(8,128)S(1)} %broadcast_maximum_fusion, pred[4,128,1024]{2,1,0:T(8,128)(4,1)S(1)} %fusion.13), kind=kLoop, calls=%fused_computation.5 | loop fusion | flops 31451136 | bytes 25739264 | tf_op jit(solution)/shard_map/reduce_sum | solution.py:121
  147.1 23.9 %all-gather.10.cloned.1.call-done = bf16[4,1024,768]{1,2,0:T(8,128)(2,1)} async-done(((bf16[4,128,768]{1,2,0:T(8,128)(2,1)}), bf16[4,1024,768]{1,2,0:T(8,128)(2,1)}) %all-gather.10.cloned.1.call-update) | async-done | bytes 6291472 | tf_op jit(solution)/shard_map/all_gather | solution.py:125
  170.9 14.2 %fusion.58 = f32[4,12,64,128]{3,2,1,0:T(8,128)} fusion(bf16[4,1024,12,64]{1,3,2,0:T(8,128)(2,1)} %bitcast.192, f32[4,12,128,1024]{3,2,1,0:T(8,128)} %get-tuple-element.76, f32[4,12,128]{2,1,0:T(8,128)S(1)} %log_add_fusion, pred[4,128,1024]{2,1,0:T(8,128)(4,1)S(1)} %fusion.13), kind=kOutput, calls=%fused_computation.110 | convolution fusion | flops 830472192 | bytes 33579008 | tf_op jit(solution)/shard_map/shqk,skhd->sqhd/dot_general | solution.py:133
  185.1 15.0 %fusion.16 = f32[4,128,12]{1,2,0:T(8,128)S(1)} fusion(f32[4,12,64,128]{3,2,1,0:T(8,128)} %fusion.58, bf16[4,1024,12,64]{1,3,2,0:T(8,128)(2,1)} %bitcast.193, f32[4,12,128,1024]{3,2,1,0:T(8,128)} %get-tuple-element.76, f32[4,12,128]{2,1,0:T(8,128)S(1)} %log_add_fusion, pred[4,128,1024]{2,1,0:T(8,128)(4,1)S(1)} %fusion.13, bf16[4,128,12,64]{1,0,3,2:T(4,128)(2,1)} %reshape.254), kind=kOutput, calls=%fused_computation.48 | convolution fusion | flops 850913280 | bytes 34390016 | tf_op jit(solution)/shard_map/shqk,skhd->sqhd/dot_general | solution.py:134
  200.2 20.5 %multiply_convert_fusion = bf16[4,12,128,1024]{3,2,1,0:T(8,128)(2,1)} fusion(f32[4,12,128,1024]{3,2,1,0:T(8,128)} %get-tuple-element.76, f32[4,12,128]{2,1,0:T(8,128)S(1)} %bitcast.198, f32[4,12,128]{2,1,0:T(8,128)S(1)} %log_add_fusion, pred[4,128,1024]{2,1,0:T(8,128)(4,1)S(1)} %fusion.13, bf16[4,1024,12,64]{1,3,2,0:T(8,128)(2,1)} %bitcast.194, ...), kind=kOutput, calls=%fused_computation.2 | convolution fusion | flops 843055104 | bytes 45400064 | tf_op jit(solution)/shard_map/sqhd,skhd->shqk/dot_general | solution.py:172
  220.6 11.1 %fusion.50 = f32[4,12,64,1024]{3,2,1,0:T(8,128)} fusion(bf16[4,12,128,1024]{3,2,1,0:T(8,128)(2,1)} %multiply_convert_fusion, bf16[4,128,12,48]{1,3,2,0:T(8,128)(2,1)S(1)} %slice.110, bf16[4,128,12,16]{1,3,2,0:T(8,128)(2,1)S(1)} %get-tuple-element.61), kind=kOutput, calls=%fused_computation.98 | convolution fusion | flops 806879232 | bytes 25952256 | tf_op jit(solution)/shard_map/shqk,sqhd->skhd/dot_general | solution.py:179
  231.8 14.7 %fusion.47 = f32[4,12,64,1024]{3,2,1,0:T(8,128)} fusion(bf16[4,128,12,64]{1,0,3,2:T(4,128)(2,1)S(1)} %copy-done.13, f32[4,12,128,1024]{3,2,1,0:T(8,128)} %get-tuple-element.76, f32[4,12,128]{2,1,0:T(8,128)S(1)} %log_add_fusion, pred[4,128,1024]{2,1,0:T(8,128)(4,1)S(1)} %fusion.13), kind=kOutput, calls=%fused_computation.94 | convolution fusion | flops 830472192 | bytes 39084032 | tf_op jit(solution)/shard_map/shqk,sqhd->skhd/dot_general | solution.py:182
  246.5 18.7 %pad_maximum_fusion.1 = f32[4,1024,1536]{1,2,0:T(8,128)} fusion(f32[4,1024,768]{1,2,0:T(8,128)} %bitcast.163, f32[4,1024,768]{1,2,0:T(8,128)} %bitcast.162), kind=kLoop, calls=%fused_computation.1 | loop fusion | flops 6291456 | bytes 50331648 | tf_op jit(solution)/shard_map/concatenate | solution.py:185
  266.0 9.5 %all-gather = bf16[8,1,384]{2,1,0:T(2,128)(2,1)S(1)} all-gather(bf16[1,1,384]{2,1,0:T(2,128)(2,1)S(1)} %reshape.280), channel_id=1, replica_groups=mesh['rep'=4,'fsdp'=8] {'fsdp'}, dimensions={0}, use_global_device_ids=true | all-gather | bytes 6912 | tf_op jit(solution)/shard_map/all_gather | solution.py:64
  276.7 8.8 fusion.83
  285.6 19.4 %convert_reduce_fusion = (f32[3072]{0:T(1024)S(1)}, bf16[512,3072]{1,0:T(8,128)(2,1)S(1)}, f32[512,3072]{1,0:T(8,128)S(1)}) fusion(f32[512,3072]{1,0:T(8,128)} %fusion.83, f32[3072]{0:T(1024)S(1)} %bitcast.190, bf16[512,768]{1,0:T(8,128)(2,1)S(1)} %bitcast.170, bf16[768,3072]{1,0:T(8,128)(2,1)} %all-gather.18.cloned.1.call-done), kind=kOutput, calls=%fused_computation.12 | convolution fusion | flops 2533880832 | bytes 21258240 | tf_op jit(solution)/shard_map/dot_general | solution.py:155
  308.2 7.8 convolution_bitcast_fusion
  321.3 11.3 %multiply_bitcast_fusion = f32[4,128,12,64]{1,3,2,0:T(8,128)S(1)} fusion(bf16[4,1024,12,64]{1,3,2,0:T(8,128)(2,1)} %bitcast.165, bf16[4,12,128,1024]{3,2,1,0:T(8,128)(2,1)} %multiply_convert_fusion), kind=kOutput, calls=%fused_computation.82 | convolution fusion | flops 805699584 | bytes 20447232 | tf_op jit(solution)/shard_map/shqk,skhd->sqhd/dot_general | solution.py:176
  340.7 82.4 %reduce-scatter.3.cloned.1.call-done = f32[4,128,1536]{1,2,0:T(8,128)} async-done(((f32[4,1024,1536]{1,2,0:T(8,128)}), f32[4,128,1536]{1,2,0:T(8,128)}) %reduce-scatter.3.cloned.1.call-update) | async-done | bytes 3145744 | tf_op jit(solution)/shard_map/reduce_scatter | solution.py:192
  436.1 19.6 %pad_maximum_fusion = f32[768,9216]{1,0:T(8,128)} fusion(f32[768,3072]{1,0:T(8,128)} %convolution_bitcast_fusion, f32[768,3072]{1,0:T(8,128)} %fusion.86, f32[768,768]{1,0:T(8,128)S(1)} %copy.57, f32[768,2304]{1,0:T(8,128)} %fusion.9), kind=kLoop, calls=%fused_computation | loop fusion | flops 21233664 | bytes 56623104 | tf_op jit(solution)/shard_map/concatenate | solution.py:239
  455.8 173.4 %reduce-scatter.5.cloned.1.call-done = f32[96,9216]{1,0:T(8,128)} async-done(((f32[768,9216]{1,0:T(8,128)}), f32[96,9216]{1,0:T(8,128)}) %reduce-scatter.5.cloned.1.call-update) | async-done | bytes 3538960 | tf_op jit(solution)/shard_map/reduce_scatter | solution.py:238
  630.9 76.9 %collective-permute-done = f32[96,9216]{1,0:T(8,128)} collective-permute-done((f32[96,9216]{1,0:T(8,128)}, f32[96,9216]{1,0:T(8,128)}, u32[]{:S(2)}, u32[]{:S(2)}) %collective-permute-start) | collective-permute-done | bytes 3538976 | tf_op jit(solution)/shard_map/ppermute | solution.py:255
  730.9 157.9 %all-reduce.18 = (f32[768]{0:T(1024)S(1)}, f32[768]{0:T(1024)S(1)}, f32[768]{0:T(1024)S(1)}, f32[768]{0:T(1024)S(1)}, f32[2304]{0:T(1024)S(1)}, /*index=5*/f32[768]{0:T(1024)S(1)}, f32[3072]{0:T(1024)S(1)}) all-reduce(f32[768]{0:T(1024)S(1)} %get-tuple-element.23, ...), channel_id=1, replica_groups=mesh['rep'=4,'fsdp'=8] {'rep','fsdp'}, use_global_device_ids=true, to_apply=%region_12.13 | all-reduce | flops 9216 | bytes 73728 | tf_op jit(solution)/shard_map/psum | solution.py:220
  (199 shorter events, 100.7 us)
Async XLA Ops:
  7.2 42.0 %all-gather.8.cloned.1.call-start = ((), (), s32[]{:S(2)}) async-start(), calls=%async_computation.2 | async-start | bytes 3981312 | tf_op jit(solution)/shard_map/all_gather | solution.py:76
  7.9 69.7 %all-gather.14.cloned.1.call-start = ((), (), s32[]{:S(2)}) async-start(), calls=%async_computation.5 | async-start | bytes 1327104 | tf_op jit(solution)/shard_map/all_gather | solution.py:138
  8.7 113.3 %all-gather.12.cloned.1.call-start = ((), (), s32[]{:S(2)}) async-start(), calls=%async_computation.4 | async-start | bytes 7077888 | tf_op jit(solution)/shard_map/all_gather | solution.py:124
  10.0 45.3 %copy-start.24 = (f32[512]{0:T(512)}, f32[512]{0:T(512)S(1)}, u32[]{:S(2)}) copy-start(f32[512]{0:T(512)S(1)} %get-tuple-element.73) | copy-start | bytes 6148
  11.6 263.9 %copy-start.28 = (f32[4,128]{1,0:T(4,128)}, f32[4,128]{1,0:T(4,128)S(1)}, u32[]{:S(2)}) copy-start(f32[4,128]{1,0:T(4,128)S(1)} %fusion.28) | copy-start | bytes 6148
  12.5 58.2 %copy-start.16 = (f32[4,128,16]{1,2,0:T(8,128)}, f32[4,128,16]{1,2,0:T(8,128)S(1)}, u32[]{:S(2)}) copy-start(f32[4,128,16]{1,2,0:T(8,128)S(1)} %get-tuple-element.67) | copy-start | bytes 98308
  12.5 58.2 %copy-start.18 = (f32[4,128,16]{1,2,0:T(8,128)}, f32[4,128,16]{1,2,0:T(8,128)S(1)}, u32[]{:S(2)}) copy-start(f32[4,128,16]{1,2,0:T(8,128)S(1)} %get-tuple-element.68) | copy-start | bytes 98308
  47.5 228.0 %copy-start.20 = (f32[768]{0:T(1024)}, f32[768]{0:T(1024)S(1)}, u32[]{:S(2)}) copy-start(f32[768]{0:T(1024)S(1)} %convert_element_type.126) | copy-start | bytes 9220
  72.8 98.2 %all-gather.10.cloned.1.call-start = ((), (), s32[]{:S(2)}) async-start(), calls=%async_computation.3 | async-start | bytes 7077888 | tf_op jit(solution)/shard_map/all_gather | solution.py:125
  75.6 201.1 %all-gather.16.cloned.1.call-start = ((), (), s32[]{:S(2)}) async-start(), calls=%async_computation.6 | async-start | bytes 5308416 | tf_op jit(solution)/shard_map/all_gather | solution.py:77
  76.2 209.3 %all-gather.18.cloned.1.call-start = ((), (), s32[]{:S(2)}) async-start(), calls=%async_computation.7 | async-start | bytes 5308416 | tf_op jit(solution)/shard_map/all_gather | solution.py:139
  76.8 346.2 %reduce-scatter.3.cloned.1.call-start = ((), (), s32[]{:S(2)}) async-start(), calls=%async_computation.8 | async-start | bytes 28311552 | tf_op jit(solution)/shard_map/reduce_scatter | solution.py:192
  265.3 363.9 %reduce-scatter.5.cloned.1.call-start = ((), (), s32[]{:S(2)}) async-start(), calls=%async_computation.9 | async-start | bytes 31850496 | tf_op jit(solution)/shard_map/reduce_scatter | solution.py:238
  285.6 19.4 %copy-start.2 = (f32[512,3072]{1,0:T(8,128)S(1)}, f32[512,3072]{1,0:T(8,128)}, u32[]{:S(2)}) copy-start(f32[512,3072]{1,0:T(8,128)} %fusion.83) | copy-start | bytes 18874372
  338.6 86.6 %copy-start.19 = (f32[4,128,16]{1,2,0:T(8,128)S(1)}, f32[4,128,16]{1,2,0:T(8,128)}, u32[]{:S(2)}) copy-start(f32[4,128,16]{1,2,0:T(8,128)} %copy-done.18) | copy-start | bytes 98308
  340.6 85.0 %copy-start.17 = (f32[4,128,16]{1,2,0:T(8,128)S(1)}, f32[4,128,16]{1,2,0:T(8,128)}, u32[]{:S(2)}) copy-start(f32[4,128,16]{1,2,0:T(8,128)} %copy-done.16) | copy-start | bytes 98308
  455.7 174.9 %copy-start.31 = (bf16[768]{0:T(1024)(128)(2,1)S(1)}, bf16[768]{0:T(1024)(128)(2,1)}, u32[]{:S(2)}) copy-start(bf16[768]{0:T(1024)(128)(2,1)} %get-tuple-element.34) | copy-start | bytes 4612
  455.7 174.9 %copy-start.30 = (bf16[768]{0:T(1024)(128)(2,1)S(1)}, bf16[768]{0:T(1024)(128)(2,1)}, u32[]{:S(2)}) copy-start(bf16[768]{0:T(1024)(128)(2,1)} %get-tuple-element.33) | copy-start | bytes 4612
  629.2 78.6 %collective-permute-start = (f32[96,9216]{1,0:T(8,128)}, f32[96,9216]{1,0:T(8,128)}, u32[]{:S(2)}, u32[]{:S(2)}) collective-permute-start(f32[96,9216]{1,0:T(8,128)} %reduce-scatter.5.cloned.1.call-done), channel_id=1, source_target_pairs={{0,8},{8,0},{16,24},{24,16},{1,9},{9,1},{17,25},{25,17},{2,10},{10... | collective-permute-start | bytes 10616840 | tf_op jit(solution)/shard_map/ppermute | solution.py:255
  630.7 84.8 %slice-start.1 = ((s8[4718592]{0:T(1024)(128)(4,1)}), s8[4194304]{0:T(1024)(128)(4,1)S(1)}, s32[]{:S(2)}) async-start(s8[4718592]{0:T(1024)(128)(4,1)} %bitcast.180), calls=%async_computation.11 | async-start | bytes 8388608
  630.8 84.7 %slice-start.2 = ((s8[4718592]{0:T(1024)(128)(4,1)}), s8[524288]{0:T(1024)(128)(4,1)S(1)}, s32[]{:S(2)}) async-start(s8[4718592]{0:T(1024)(128)(4,1)} %bitcast.180), calls=%async_computation.12 | async-start | bytes 1048576
  630.9 84.7 %copy-start.9 = (bf16[512,3072]{1,0:T(8,128)(2,1)S(1)}, bf16[512,3072]{1,0:T(8,128)(2,1)}, u32[]{:S(2)}) copy-start(bf16[512,3072]{1,0:T(8,128)(2,1)} %copy-done.8) | copy-start | bytes 9437188
  713.1 182.5 %collective-permute-start.1 = (f32[96,9216]{1,0:T(8,128)}, f32[96,9216]{1,0:T(8,128)}, u32[]{:S(2)}, u32[]{:S(2)}) collective-permute-start(f32[96,9216]{1,0:T(8,128)} %add.201), channel_id=1, source_target_pairs={{0,16},{8,24},{16,0},{24,8},{1,17},{9,25},{17,1},{25,9},{2,18},{10... | collective-permute-start | bytes 10616840 | tf_op jit(solution)/shard_map/ppermute | solution.py:255
  888.9 13.4 %copy-start.34 = (f32[96]{0:T(128)}, f32[96]{0:T(128)S(1)}, u32[]{:S(2)}) copy-start(f32[96]{0:T(128)S(1)} %dynamic_slice.26) | copy-start | bytes 1156
  (26 other events, 116.8 us)
Sparse Core Ops, SparseCore 0:
  9.9 36.8 all-gather.7
  48.7 24.0 all-gather.13
  75.2 46.6 all-gather.11
  124.2 46.6 all-gather.9
  172.7 38.9 all-gather.15
  213.4 38.9 all-gather.17
  265.4 157.5 reduce-scatter.2
  455.9 173.2 reduce-scatter.4
